TPU v7x, 32 devices: a whole 2x2x4 slice. The times are simulated.
32 devices in a mesh: seq: 4 (over z), enc: 4 (over y, core), head: 2 (over x).
Axes of the slice: x: 2, y: 2, z: 4, core: 2. Of those that a mesh axis runs over, the one named last changes fastest.
Arguments:
- mel_frames: bfloat16 [8192, 128], P(('seq', 'enc')), may hold values from -6 to 6
- conv_weight: bfloat16 [384, 1280], replicated, may hold values from -0.3125 to 0.3125
- conv_bias: float32 [1280], replicated, may hold values from -3 to 3
- projector: bfloat16 [1280, 4, 512], P(None, None, 'head'), may hold values from -0.15625 to 0.15625
- seg_offsets: int32 [8], replicated, may hold values from 0 to 8191, as said below
- seg_lengths: int32 [8], replicated, may hold values from 1 to 1535, as said below
- text_embed: bfloat16 [8192, 2048], P('seq', ('enc', 'head')), may hold values from -6 to 6
- mix_taps: float32 [4, 2048], P(None, ('enc', 'head')), may hold values from -3 to 3
- input_map: bfloat16 [8192, 512], P('seq', 'enc'), may hold values from -1.796875 to 1.796875
- output_map: bfloat16 [8192, 512], P('seq', 'enc'), may hold values from -1.796875 to 1.796875
- step_size: float32 [32, 8192], P(('enc', 'head'), 'seq'), may hold values from 0 to 2, as said below
- decay_log: float32 [32], P(('enc', 'head')), may hold values from -6 to -2
- skip_gain: float32 [32], P(('enc', 'head')), may hold values from 0.5 to 1.5
Outputs:
- mixer_out: bfloat16 [8192, 2048], P('seq', ('enc', 'head'))
Inputs may be any that keep to these rules, and one draw needn't show every extreme that they name: `seg_offsets`: offsets rise; owner k's two segments lie within positions k * 2048 to (k+1) * 2048 - 1 without intersection. Owner k's audio tokens are those of track indices within 256 of k * 1024 to (k+1) * 1024 - 1; in every draw some owner takes 256 tokens from each neighbour's share. `seg_lengths`: the lengths sum to 4096; an owner's two segments together hold between 512 and 1536 tokens. `step_size`: Positive.
All inputs are finite; a program needn't handle non-finite values.
Results may differ from a plain program's by a relative error of at most 0.006.
Values may be sent and summed in bfloat16 or wider, within the bound.
A program may use at most 64 MiB of HBM per device.

v0:
```python
import jax
import jax.numpy as jnp
from jax import lax
from jax.sharding import PartitionSpec as P

HDIM = 64
SPAN = 128
DRIFT = 256


highest = lax.Precision.HIGHEST
high_mode = lax.Precision.HIGH


def from_behind(value, axis, by):
    count = lax.axis_size(axis)
    pairs = [(i, i + by) for i in range(count) if 0 <= i + by < count]
    return lax.ppermute(value, axis, pairs)


def padded_2(block, sides, width):
    for axis, dim in sides:
        count = lax.axis_size(axis)
        forward = [(i, i + 1) for i in range(count - 1)]
        backward = [(target, source) for source, target in forward]
        low = lax.ppermute(
            lax.slice_in_dim(block, block.shape[dim] - width, None, axis=dim), axis, forward
        )
        high = lax.ppermute(lax.slice_in_dim(block, 0, width, axis=dim), axis, backward)
        block = jnp.concatenate([low, block, high], axis=dim)
    return block


def entering(value, axis, join, neutral):
    place = lax.axis_index(axis)
    gathered = jax.tree.map(
        lambda a, kind: lax.all_gather(a.astype(kind), axis), value, (jnp.bfloat16, jnp.bfloat16)
    )
    state = jax.tree.map(lambda a, e: jnp.zeros_like(a) + jnp.asarray(e, a.dtype), value, neutral)

    def one(hop, state):
        return join(
            state,
            jax.tree.map(
                lambda a, own: lax.dynamic_index_in_dim(a, hop, 0, False).astype(own.dtype),
                gathered,
                value,
            ),
        )

    return lax.fori_loop(0, place, one, state)


def shards(
    mel_frames,
    conv_weight,
    conv_bias,
    projector,
    seg_offsets,
    seg_lengths,
    text_embed,
    mix_taps,
    input_map,
    output_map,
    step_size,
    decay_log,
    skip_gain,
):
    tiles = mel_frames.shape[0] // 2
    channels = mel_frames.shape[1]
    enc_count = lax.axis_size("enc")
    tile_first = (lax.axis_index("seq") * enc_count + lax.axis_index("enc")) * tiles
    seg_start = jnp.cumsum(seg_lengths) - seg_lengths
    frame_pairs = mel_frames.reshape(tiles, 2 * channels)
    edge_frame = from_behind(frame_pairs[-1:, channels:], ("seq", "enc"), 1)
    tokens = tile_first + jnp.arange(tiles, dtype=jnp.int32)
    opening = jnp.any(tokens[:, None] == seg_start[None, :], axis=1)
    left_frames = jnp.concatenate([edge_frame, frame_pairs[:-1, channels:]], axis=0)
    left_frames = jnp.where(opening[:, None], jnp.zeros_like(left_frames), left_frames)
    stacked = jnp.concatenate([left_frames, frame_pairs], axis=1)
    summed = jnp.dot(stacked, conv_weight, preferred_element_type=jnp.float32) + conv_bias
    features = jax.nn.gelu(summed, approximate=False).astype(jnp.bfloat16)
    column_width = projector.shape[2]
    projected = jnp.dot(
        features, projector.reshape(projector.shape[0], -1), preferred_element_type=jnp.float32
    )
    projected = projected.astype(jnp.bfloat16).reshape(tiles, enc_count, column_width)
    audio_rows = lax.all_to_all(projected, "enc", split_axis=1, concat_axis=0, tiled=True).reshape(
        tiles * enc_count, column_width
    )
    shard_audio = audio_rows.shape[0]
    widened = padded_2(audio_rows, (("seq", 0),), DRIFT)
    row_count = text_embed.shape[0]
    owner_index = lax.axis_index("seq")
    places = owner_index * row_count + jnp.arange(row_count, dtype=jnp.int32)
    segment = jnp.sum((places[:, None] >= seg_offsets[None, :]).astype(jnp.int32), axis=1) - 1
    chosen = jnp.arange(seg_offsets.shape[0], dtype=jnp.int32)[None, :] == segment[:, None]
    offset_here = jnp.sum(jnp.where(chosen, seg_offsets[None, :], 0), axis=1)
    length_here = jnp.sum(jnp.where(chosen, seg_lengths[None, :], 0), axis=1)
    start_here = jnp.sum(jnp.where(chosen, seg_start[None, :], 0), axis=1)
    within = places - offset_here
    is_audio = (segment >= 0) & (within < length_here)
    local_row = jnp.where(is_audio, start_here + within - owner_index * shard_audio + DRIFT, 0)
    x_raw = jnp.where(is_audio[:, None], jnp.take(widened, local_row, axis=0), text_embed)
    previous = from_behind(x_raw[-3:], "seq", 1)
    padded = jnp.concatenate([previous, x_raw], axis=0)
    summed_mix = jnp.zeros(x_raw.shape, jnp.float32)
    for offset in range(4):
        summed_mix = (
            summed_mix + padded[offset : offset + row_count].astype(jnp.float32) * mix_taps[offset]
        )
    mixed_in = jax.nn.silu(summed_mix).astype(jnp.bfloat16)
    head_count = step_size.shape[0]
    blocks = row_count // SPAN
    plain = mixed_in.reshape(blocks, SPAN, head_count, HDIM)
    values = plain.astype(jnp.float32)
    b_rows = input_map.reshape(blocks, SPAN, -1)
    c_rows = output_map.reshape(blocks, SPAN, -1)
    b_all = b_rows.astype(jnp.float32)
    c_all = c_rows.astype(jnp.float32)
    step_sizes = step_size.T.reshape(blocks, SPAN, head_count)
    log_decay = -step_sizes * jnp.exp(decay_log)[None, None, :]
    running = jnp.cumsum(log_decay, axis=1)
    lower_mask = (jnp.arange(SPAN)[:, None] >= jnp.arange(SPAN)[None, :])[None, :, :, None]
    gap_logs = running[:, :, None, :] - running[:, None, :, :]
    decay_table = jnp.where(lower_mask, jnp.exp(jnp.where(lower_mask, gap_logs, 0.0)), 0.0)
    intersection = jnp.einsum("cin,cjn->cij", c_rows, b_rows, preferred_element_type=jnp.float32)
    weight = (decay_table * intersection[..., None] * step_sizes[:, None, :, :]).astype(
        jnp.bfloat16
    )
    inner_part = jnp.einsum("cijh,cjhp->cihp", weight, plain, preferred_element_type=jnp.float32)
    inputs = values * step_sizes[..., None]
    tail_decay = jnp.exp(running[:, -1:, :] - running)
    block_states = jnp.einsum(
        "cjhp,cjn->chpn", inputs * tail_decay[..., None], b_all, precision=high_mode
    )
    totals = running[:, -1, :]
    through = jnp.cumsum(totals, axis=0)
    before_block = through - totals
    block_order = jnp.arange(blocks)
    earlier = (block_order[None, :] < block_order[:, None])[:, :, None]
    weights = jnp.where(
        earlier,
        jnp.exp(jnp.where(earlier, before_block[:, None, :] - through[None, :, :], 0.0)),
        0.0,
    )
    local_starts = jnp.einsum("cdh,dhpn->chpn", weights, block_states, precision=highest)
    device_total = through[-1]
    device_state = jnp.einsum(
        "dh,dhpn->hpn", jnp.exp(device_total[None, :] - through), block_states, precision=highest
    )

    def combine(earlier_part, later_part):
        return (
            earlier_part[0] + later_part[0],
            earlier_part[1] * jnp.exp(later_part[0])[:, None, None] + later_part[1],
        )

    identity = (jnp.zeros_like(device_total), jnp.zeros_like(device_state))
    passed_total, incoming = entering((device_total, device_state), "seq", combine, identity)
    block_in = local_starts + jnp.exp(before_block)[:, :, None, None] * incoming[None]
    carried = (
        jnp.einsum("cin,chpn->cihp", c_all, block_in, precision=high_mode)
        * jnp.exp(running)[..., None]
    )
    output = inner_part + carried + skip_gain[None, None, :, None] * values
    return output.reshape(row_count, head_count * HDIM).astype(jnp.bfloat16)


def solution(mesh):
    return jax.shard_map(
        shards,
        mesh=mesh,
        in_specs=(
            P(("seq", "enc"), None),
            P(),
            P(),
            P(None, None, "head"),
            P(),
            P(),
            P("seq", ("enc", "head")),
            P(None, ("enc", "head")),
            P("seq", "enc"),
            P("seq", "enc"),
            P(("enc", "head"), "seq"),
            P(("enc", "head")),
            P(("enc", "head")),
        ),
        out_specs=P("seq", ("enc", "head")),
        check_vma=False,
    )
```

profile of v0, /device:TPU:0, one launch (start us, length us, event | category | flops | bytes accessed | tf_op | source)
XLA Modules:
  0.0 116.1 jit_solution(5086975355669025590)
XLA Ops:
  1.1 2.4 %collective-permute-start = (bf16[1,128]{1,0:T(2,128)(2,1)S(1)}, bf16[1,128]{1,0:T(2,128)(2,1)S(1)}, u32[]{:S(2)}, u32[]{:S(2)}) collective-permute-start(bf16[1,128]{1,0:T(2,128)(2,1)S(1)} %slice.67), channel_id=1, source_target_pairs={{0,2},{2,4},{4,6},{6,8},{8,10},{10,12},{12,14},{14,16},{16,18},{18... | collective-permute-start | bytes 776 | tf_op jit(solution)/shard_map/ppermute | solution.py:18
  9.3 2.7 %fusion.124 = f32[16,128,128]{2,1,0:T(8,128)} fusion(bf16[16,128,128]{2,1,0:T(8,128)(2,1)} %bitcast.103, bf16[16,128,128]{2,1,0:T(8,128)(2,1)} %bitcast.101), kind=kOutput, calls=%fused_computation.171 | convolution fusion | flops 67108864 | bytes 2097152 | tf_op jit(solution)/shard_map/cin,cjn->cij/dot_general | solution.py:127
  12.0 3.9 %copy.133 = bf16[160,8,4,256]{3,1,2,0:T(8,128)(2,1)} copy(bf16[160,8,4,256]{3,2,1,0:T(4,128)(2,1)} %bitcast.99) | data formatting | bytes 5242880
  16.0 5.7 %convolution_convert_fusion = bf16[256,1024]{1,0:T(8,128)(2,1)S(1)} fusion(bf16[1280,1024]{1,0:T(8,128)(2,1)} %bitcast.100, bf16[384,1280]{1,0:T(8,128)(2,1)S(1)} %copy-done, f32[1280]{0:T(1024)S(1)} %copy-done.6, bf16[256,256]{1,0:T(8,128)(2,1)S(1)} %reshape.210, bf16[256,128]{1,0:T(8,128)(2,1)S(1)} %maximum_select_fusion), kind=kOutput, calls=%fused_computation.49 | convolution fusion | flops 945029120 | bytes 4330496 | tf_op jit(solution)/shard_map/dot_general | solution.py:84
  22.5 5.0 %all-to-all-start = ((bf16[256,4,256]{2,0,1:T(8,128)(2,1)}), bf16[256,4,256]{2,0,1:T(8,128)(2,1)S(1)}, u32[]{:S(2)}, u32[]{:S(2)}) async-start(bf16[256,4,256]{2,0,1:T(8,128)(2,1)} %bitcast.90), calls=%async_computation | async-start | bytes 1048576 | tf_op jit(solution)/shard_map/all_to_all | solution.py:88
  29.2 7.6 %all-to-all-done = bf16[256,4,256]{2,0,1:T(8,128)(2,1)S(1)} async-done(((bf16[256,4,256]{2,0,1:T(8,128)(2,1)}), bf16[256,4,256]{2,0,1:T(8,128)(2,1)S(1)}, u32[]{:S(2)}, u32[]{:S(2)}) %all-to-all-start) | async-done | bytes 524320 | tf_op jit(solution)/shard_map/all_to_all | solution.py:88
  36.8 3.5 %collective-permute-start.1 = (bf16[256,256]{1,0:T(8,128)(2,1)S(1)}, bf16[256,256]{1,0:T(8,128)(2,1)S(1)}, u32[]{:S(2)}, u32[]{:S(2)}) collective-permute-start(bf16[256,256]{1,0:T(8,128)(2,1)S(1)} %get-tuple-element.68), channel_id=1, source_target_pairs={{0,8},{8,16},{16,24},{1,9},{9,17},{17,25},{2,10},{10,18},{18,26},{... | collective-permute-start | bytes 393224 | tf_op jit(solution)/shard_map/ppermute | solution.py:26
  43.2 4.1 %collective-permute-done.2 = bf16[256,256]{1,0:T(8,128)(2,1)S(1)} collective-permute-done((bf16[256,256]{1,0:T(8,128)(2,1)S(1)}, bf16[256,256]{1,0:T(8,128)(2,1)S(1)}, u32[]{:S(2)}, u32[]{:S(2)}) %collective-permute-start.2) | collective-permute-done | bytes 131104 | tf_op jit(solution)/shard_map/ppermute | solution.py:29
  47.4 9.1 %gather_fusion = bf16[2048,256]{1,0:T(8,128)(2,1)} fusion(bf16[1536,256]{1,0:T(8,128)(2,1)S(1)} %pad_maximum_fusion.1, s32[2048]{0:T(1024)S(1)} %broadcast_clamp_fusion), kind=kCustom, calls=%fused_computation | custom fusion | bytes 2105344 | tf_op jit(solution)/shard_map/jit(_take)/gather | solution.py:104
  56.4 3.1 %select_select_fusion = bf16[2048,256]{1,0:T(8,128)(2,1)S(1)} fusion(bf16[2048,256]{1,0:T(8,128)(2,1)} %param.21, bf16[2048,256]{1,0:T(8,128)(2,1)} %gather_fusion, pred[2048]{0:T(1024)(128)(4,1)S(1)} %get-tuple-element.63, pred[2048]{0:T(1024)(128)(4,1)S(1)} %get-tuple-element.64), kind=kLoop, calls=%fused_computation.59 | loop fusion | flops 1048576 | bytes 3149824 | tf_op jit(solution)/shard_map/jit(_where)/select_n | solution.py:104
  59.6 3.5 %collective-permute-start.3 = (bf16[3,256]{1,0:T(4,128)(2,1)S(1)}, bf16[3,256]{1,0:T(4,128)(2,1)S(1)}, u32[]{:S(2)}, u32[]{:S(2)}) collective-permute-start(bf16[3,256]{1,0:T(4,128)(2,1)S(1)} %slice.71), channel_id=1, source_target_pairs={{0,8},{8,16},{16,24},{1,9},{9,17},{17,25},{2,10},{10,18},{18,26},{... | collective-permute-start | bytes 4616 | tf_op jit(solution)/shard_map/ppermute | solution.py:18
  63.1 8.2 %all-gather.1 = bf16[4,1,4]{2,1,0:T(2,128)(2,1)S(1)} all-gather(bf16[1,1,4]{2,1,0:T(2,128)(2,1)S(1)} %convert_bitcast_fusion), channel_id=1, replica_groups=mesh['seq'=4,'enc'=4,'head'=2] {'seq'}, dimensions={0}, use_global_device_ids=true | all-gather | bytes 40 | tf_op jit(solution)/shard_map/all_gather | solution.py:37
  72.3 1.7 %copy.110 = f32[16,128,4]{1,2,0:T(4,128)S(1)} copy(f32[16,128,4]{2,0,1:T(8,128)} %get-tuple-element.67) | data formatting | bytes 65536 | tf_op jit(solution)/shard_map/exp | solution.py:133
  75.2 2.3 %multiply_convert_fusion.2 = bf16[2048,256]{1,0:T(8,128)(2,1)} fusion(bf16[2048,256]{1,0:T(8,128)(2,1)S(1)} %select_select_fusion, bf16[3,256]{1,0:T(4,128)(2,1)S(1)} %collective-permute-done.3, f32[256]{0:T(256)S(1)} %bitcast.119, f32[256]{0:T(256)S(1)} %bitcast.120, f32[256]{0:T(256)S(1)} %bitcast.118, f32[256]{0:T(256)S(1)} %bitcast.117), kind=kLoop, calls=%fused_computation.22 | loop fusion | flops 13107200 | bytes 2102784 | tf_op jit(solution)/shard_map/convert_element_type | solution.py:112
  77.4 3.3 %reshape.236 = bf16[16,128,4,64]{3,2,1,0:T(4,128)(2,1)S(1)} reshape(bf16[2048,256]{1,0:T(8,128)(2,1)} %multiply_convert_fusion.2) | data formatting | bytes 2097152 | tf_op jit(solution)/shard_map/reshape | solution.py:115
  80.8 2.1 %copy.105 = bf16[16,128,4,64]{1,3,2,0:T(8,128)(2,1)} copy(bf16[16,128,4,64]{3,2,1,0:T(4,128)(2,1)S(1)} %reshape.236) | data formatting | bytes 2097152 | tf_op jit(solution)/shard_map/reshape | solution.py:115
  82.9 2.1 %fusion.2 = f32[16,4,64,128]{3,2,1,0:T(8,128)S(1)} fusion(bf16[16,128,128,1]{2,1,3,0:T(8,128)(2,1)} %bitcast.102, bf16[16,128,4,64]{1,3,2,0:T(8,128)(2,1)} %copy.105, f32[16,128,4]{1,2,0:T(4,128)S(1)} %copy.110, f32[16,128,4]{1,2,0:T(4,128)S(1)} %bitcast.109), kind=kOutput, calls=%fused_computation.9 | convolution fusion | flops 404226048 | bytes 3735552 | tf_op jit(solution)/shard_map/cjhp,cjn->chpn/dot_general | solution.py:134
  85.0 2.2 %fusion.15 = f32[4,1,64,128]{3,1,2,0:T(1,128)S(1)} fusion(f32[16,4,1,1]{0,2,3,1:T(1,128)S(1)} %copy.123, f32[16,4,64,128]{3,2,1,0:T(8,128)S(1)} %fusion.2), kind=kOutput, calls=%fused_computation.24 | convolution fusion | flops 6291456 | bytes 2228480 | tf_op jit(solution)/shard_map/dh,dhpn->hpn/dot_general | solution.py:149
  87.3 13.8 %all-gather = bf16[16,64,128]{2,1,0:T(8,128)(2,1)S(1)} all-gather(bf16[4,64,128]{2,1,0:T(8,128)(2,1)S(1)} %convert_element_type.72), channel_id=2, replica_groups=mesh['seq'=4,'enc'=4,'head'=2] {'seq'}, dimensions={0}, use_global_device_ids=true | all-gather | bytes 327680 | tf_op jit(solution)/shard_map/all_gather | solution.py:37
  101.3 3.9 %fusion = f32[16,4,64,128]{3,2,1,0:T(8,128)S(1)} fusion(bf16[16,128,4,64]{1,3,2,0:T(8,128)(2,1)} %copy.105, f32[16,128,4]{1,2,0:T(4,128)S(1)} %bitcast.110, f32[16,128,128]{2,1,0:T(8,128)} %fusion.124, f32[16,128,4]{1,2,0:T(4,128)} %copy.102, pred[128,128]{1,0:T(8,128)(4,1)} %iota_compare_fusion), kind=kOutput, calls=%fused_computation.7 | convolution fusion | flops 140509184 | bytes 4276224 | tf_op jit(solution)/shard_map/cijh,cjhp->cihp/dot_general | solution.py:131
  105.2 3.2 %bitcast_add_fusion = f32[16,4,64,128]{3,0,2,1:T(8,128)S(1)} fusion(f32[16,4,64,128]{3,2,1,0:T(8,128)S(1)} %fusion.2, f32[4,64,128]{2,1,0:T(8,128)S(1)} %get-tuple-element.49, f32[16,4]{0,1:T(4,128)S(1)} %copy.116, f32[16,4]{0,1:T(4,128)S(1)} %copy.112, f32[16,4]{0,1:T(4,128)S(1)} %fusion.87, pred[16,16]{1,0:T(8,128)(4,1)S(1)} %iota_compare_fusion.2), kind=kOutput, calls=%fused_computation.14 | convolution fusion | flops 101714944 | bytes 4326400 | tf_op jit(solution)/shard_map/cdh,dhpn->chpn/dot_general | solution.py:147
  108.5 2.6 %fusion.5 = bf16[16,128,4,64]{1,3,2,0:T(8,128)(2,1)} fusion(bf16[16,128,4,64]{1,3,2,0:T(8,128)(2,1)S(1)} %copy-done.1, f32[16,4,64,128]{3,2,1,0:T(8,128)S(1)} %fusion, bf16[16,128,128,1]{2,1,3,0:T(8,128)(2,1)S(1)} %bitcast.104, f32[16,4,64,128]{3,0,2,1:T(8,128)S(1)} %bitcast_add_fusion, f32[4]{0:T(128)S(1)} %copy-done.5, f32[16,128,4]{1,2,0:T(4,128)S(1)} %copy.118), kind=kOutput, calls=%fused_computation.11 | convolution fusion | flops 405798912 | bytes 6848528 | tf_op jit(solution)/shard_map/cin,chpn->cihp/dot_general | solution.py:163
  111.1 2.9 %copy.126 = bf16[16,128,4,64]{3,2,1,0:T(4,128)(2,1)S(1)} copy(bf16[16,128,4,64]{1,3,2,0:T(8,128)(2,1)} %fusion.5) | data formatting | bytes 2097152 | tf_op jit(solution)/shard_map/convert_element_type | solution.py:167
  114.0 2.2 %reshape.235 = bf16[2048,256]{1,0:T(8,128)(2,1)} reshape(bf16[16,128,4,64]{3,2,1,0:T(4,128)(2,1)S(1)} %copy.126) | data formatting | bytes 2097152 | tf_op jit(solution)/shard_map/convert_element_type | solution.py:167
  (64 shorter events, 14.8 us)
Async XLA Ops:
  0.0 16.0 %copy-start = (bf16[384,1280]{1,0:T(8,128)(2,1)S(1)}, bf16[384,1280]{1,0:T(8,128)(2,1)}, u32[]{:S(2)}) copy-start(bf16[384,1280]{1,0:T(8,128)(2,1)} %param.16) | copy-start | bytes 2949124
  0.0 8.8 %copy-start.7 = (f32[4]{0:T(128)S(1)}, f32[4]{0:T(128)}, u32[]{:S(2)}) copy-start(f32[4]{0:T(128)} %param.26) | copy-start | bytes 52
  1.1 14.8 %collective-permute-start = (bf16[1,128]{1,0:T(2,128)(2,1)S(1)}, bf16[1,128]{1,0:T(2,128)(2,1)S(1)}, u32[]{:S(2)}, u32[]{:S(2)}) collective-permute-start(bf16[1,128]{1,0:T(2,128)(2,1)S(1)} %slice.67), channel_id=1, source_target_pairs={{0,2},{2,4},{4,6},{6,8},{8,10},{10,12},{12,14},{14,16},{16,18},{18... | collective-permute-start | bytes 776 | tf_op jit(solution)/shard_map/ppermute | solution.py:18
  12.0 4.0 %copy-start.6 = (f32[1280]{0:T(1024)S(1)}, f32[1280]{0:T(1024)}, u32[]{:S(2)}) copy-start(f32[1280]{0:T(1024)} %param.17) | copy-start | bytes 15364
  22.5 14.3 %all-to-all-start = ((bf16[256,4,256]{2,0,1:T(8,128)(2,1)}), bf16[256,4,256]{2,0,1:T(8,128)(2,1)S(1)}, u32[]{:S(2)}, u32[]{:S(2)}) async-start(bf16[256,4,256]{2,0,1:T(8,128)(2,1)} %bitcast.90), calls=%async_computation | async-start | bytes 1048576 | tf_op jit(solution)/shard_map/all_to_all | solution.py:88
  36.8 6.4 %collective-permute-start.1 = (bf16[256,256]{1,0:T(8,128)(2,1)S(1)}, bf16[256,256]{1,0:T(8,128)(2,1)S(1)}, u32[]{:S(2)}, u32[]{:S(2)}) collective-permute-start(bf16[256,256]{1,0:T(8,128)(2,1)S(1)} %get-tuple-element.68), channel_id=1, source_target_pairs={{0,8},{8,16},{16,24},{1,9},{9,17},{17,25},{2,10},{10,18},{18,26},{... | collective-permute-start | bytes 393224 | tf_op jit(solution)/shard_map/ppermute | solution.py:26
  40.3 7.0 %collective-permute-start.2 = (bf16[256,256]{1,0:T(8,128)(2,1)S(1)}, bf16[256,256]{1,0:T(8,128)(2,1)S(1)}, u32[]{:S(2)}, u32[]{:S(2)}) collective-permute-start(bf16[256,256]{1,0:T(8,128)(2,1)S(1)} %get-tuple-element.69), channel_id=1, source_target_pairs={{8,0},{16,8},{24,16},{9,1},{17,9},{25,17},{10,2},{18,10},{26,18},{... | collective-permute-start | bytes 393224 | tf_op jit(solution)/shard_map/ppermute | solution.py:29
  59.6 15.6 %collective-permute-start.3 = (bf16[3,256]{1,0:T(4,128)(2,1)S(1)}, bf16[3,256]{1,0:T(4,128)(2,1)S(1)}, u32[]{:S(2)}, u32[]{:S(2)}) collective-permute-start(bf16[3,256]{1,0:T(4,128)(2,1)S(1)} %slice.71), channel_id=1, source_target_pairs={{0,8},{8,16},{16,24},{1,9},{9,17},{17,25},{2,10},{10,18},{18,26},{... | collective-permute-start | bytes 4616 | tf_op jit(solution)/shard_map/ppermute | solution.py:18
  72.3 2.4 %copy-start.2 = (f32[16,128,4]{2,0,1:T(8,128)S(1)}, f32[16,128,4]{2,0,1:T(8,128)}, u32[]{:S(2)}) copy-start(f32[16,128,4]{2,0,1:T(8,128)} %get-tuple-element.66) | copy-start | bytes 98308
  80.7 2.2 %copy-start.4 = (f32[4,2048]{1,0:T(4,128)S(1)}, f32[4,2048]{1,0:T(4,128)}, u32[]{:S(2)}) copy-start(f32[4,2048]{1,0:T(4,128)} %param.25) | copy-start | bytes 98308
  105.2 3.2 %copy-start.1 = (bf16[16,128,4,64]{1,3,2,0:T(8,128)(2,1)S(1)}, bf16[16,128,4,64]{1,3,2,0:T(8,128)(2,1)}, u32[]{:S(2)}) copy-start(bf16[16,128,4,64]{1,3,2,0:T(8,128)(2,1)} %copy.105) | copy-start | bytes 3145732
  105.2 3.2 %copy-start.3 = (bf16[2048,128]{1,0:T(8,128)(2,1)S(1)}, bf16[2048,128]{1,0:T(8,128)(2,1)}, u32[]{:S(2)}) copy-start(bf16[2048,128]{1,0:T(8,128)(2,1)} %param.24) | copy-start | bytes 1572868
  105.2 3.2 %copy-start.5 = (f32[4]{0:T(128)S(1)}, f32[4]{0:T(128)}, u32[]{:S(2)}) copy-start(f32[4]{0:T(128)} %param.27) | copy-start | bytes 52
where the time goes:
time: 117 us; the launch traced here: 116 us
  local copies, waits for them, and re-layouts  31.7 us (27%)
  matrix products  22.4 us (19%)
  blocking collectives  22 us (19%)
  starting transfers between devices  15.6 us (13%)
  waiting for transfers between devices  12.7 us (11%)
  other arithmetic  11.2 us (10%)
    all_gather x2, blocking collectives, entering(): lax.all_gather(a.astype(kind), axis)  22 us
    gather x1, local copies, waits for them, and re-layouts, shards(): jnp.take(widened, local_row, axis=0)  9.06 us
    all_to_all x1, waiting for transfers between devices, shards(): lax.all_to_all(projected, 'enc', split_axis=1, concat_axis=0, tiled=True)  7.61 us
    ppermute x2, starting transfers between devices, from_behind(): return lax.ppermute(value, axis, pairs)  5.83 us
    dot_general x1, matrix products, shards(): jnp.dot(features, projector.reshape(projector.shape[0], -1), preferred_el...  5.66 us
    reshape x2, local copies, waits for them, and re-layouts, shards(): plain = mixed_in.reshape(blocks, SPAN, head_count, HDIM)  5.45 us
    unnamed x21, local copies, waits for them, and re-layouts  5.3 us
    all_to_all x1, starting transfers between devices, shards(): lax.all_to_all(projected, 'enc', split_axis=1, concat_axis=0, tiled=True)  5.03 us
  transfers between devices with their start and end apart: 5, of which 3 were waited for; matrix products, arithmetic and copies ran while one was open for 16% of the time, Pallas kernels for 0%

commit v1 on v0

v1 whole, which is shorter than its diff:
```python
import functools

import jax
import jax.numpy as jnp
from jax import lax
from jax.experimental import pallas as pl
from jax.experimental.pallas import tpu as pltpu
from jax.sharding import PartitionSpec as P

HDIM = 64
SPAN = 128
DRIFT = 256
TAIL = 16
PLACED = 256
FRONT = DRIFT + TAIL
MESH = pl.DeviceIdType.MESH
F32 = jnp.float32
BF16 = jnp.bfloat16


def kernel(
    owners,
    encs,
    seg_off,
    seg_len,
    mel,
    conv_w,
    bias,
    proj,
    text,
    taps,
    b_map,
    c_map,
    step,
    params,
    out,
    mel_f,
    edge,
    text_tail,
    feat,
    sent,
    wide,
    x_rows,
    xconv,
    step_s,
    run_s,
    weights,
    state,
    starts,
    before_s,
    y_s,
    mine,
    mine_total,
    states,
    totals,
    edge_sems,
    tail_sems,
    enc_send,
    enc_recv,
    front_send,
    front_recv,
    back_send,
    back_recv,
    state_send,
    state_recv,
    total_send,
    total_recv,
):
    s = lax.axis_index("seq")
    e = lax.axis_index("enc")
    frames = mel.shape[0]
    tiles = frames // 2
    share = encs * tiles
    rows, width = text.shape
    blocks = rows // SPAN
    heads = step.shape[0]
    halves = width // SPAN
    flat = s * encs + e
    segments = seg_off.shape[0]

    barrier = pltpu.get_barrier_semaphore()

    def greet(device):
        pl.semaphore_signal(barrier, inc=1, device_id=device, device_id_type=MESH)

    for j in range(1, encs):
        greet({"enc": lax.rem(e + j, encs)})

    @pl.when(s > 0)
    def _():
        for j in range(encs):
            greet({"seq": s - 1, "enc": j})

    @pl.when(s < owners - 1)
    def _():
        for j in range(encs):
            greet({"seq": s + 1, "enc": j})

    def greet_far(r, carry):
        @pl.when((r > s + 1) | (r < s - 1))
        def _():
            greet({"seq": r})

        return carry

    lax.fori_loop(0, owners, greet_far, 0)
    beside = (s > 0).astype(jnp.int32) + (s < owners - 1).astype(jnp.int32)
    pl.semaphore_wait(barrier, encs - 1 + beside * encs + owners - 1 - beside)

    edge_copy = pltpu.make_async_remote_copy(
        src_ref=mel.at[pl.ds(frames - TAIL, TAIL)],
        dst_ref=edge,
        send_sem=edge_sems.at[0],
        recv_sem=edge_sems.at[1],
        device_id={"seq": (flat + 1) // encs, "enc": lax.rem(e + 1, encs)},
        device_id_type=MESH,
    )
    tail_copy = pltpu.make_async_remote_copy(
        src_ref=text.at[pl.ds(rows - TAIL, TAIL)],
        dst_ref=text_tail,
        send_sem=tail_sems.at[0],
        recv_sem=tail_sems.at[1],
        device_id={"seq": s + 1},
        device_id_type=MESH,
    )

    @pl.when(flat < owners * encs - 1)
    def _():
        edge_copy.start()

    @pl.when(s < owners - 1)
    def _():
        tail_copy.start()

    step_s[...] = jnp.zeros_like(step_s)
    for c in range(blocks):
        step_s[c * 8 : c * 8 + heads, :] = step[:, c * SPAN : (c + 1) * SPAN]
    rate = params[0:8, 0:SPAN]
    logs = -(step_s[...].reshape(blocks, 8, SPAN) * rate[None]).reshape(blocks * 8, SPAN)
    row_ids = lax.broadcasted_iota(jnp.int32, (SPAN, SPAN), 0)
    lane_ids = lax.broadcasted_iota(jnp.int32, (SPAN, SPAN), 1)
    upper = (row_ids <= lane_ids).astype(F32)
    run_s[...] = jnp.dot(
        logs, upper, preferred_element_type=F32, precision=lax.Precision.HIGHEST
    )

    mel_f[8:, :] = mel[...].astype(F32)

    @pl.when(flat == 0)
    def _():
        mel_f[0:8, :] = jnp.zeros((8, mel.shape[1]), F32)

    tokens = flat * tiles + lax.broadcasted_iota(jnp.int32, (tiles, SPAN), 0)

    def opens(k, carry):
        begin, hit = carry
        return begin + seg_len[k], jnp.where(tokens == begin, 1, hit)

    _, opening = lax.fori_loop(
        0, segments, opens, (jnp.int32(0), jnp.zeros((tiles, SPAN), jnp.int32))
    )

    @pl.when(flat > 0)
    def _():
        edge_copy.wait_recv()
        mel_f[0:8, :] = edge[...].astype(F32)[TAIL - 8 :, :]

    left = jnp.where(opening > 0, 0.0, mel_f[pl.ds(7, tiles, stride=2), :])
    stacked = jnp.concatenate(
        [left, mel_f[pl.ds(8, tiles, stride=2), :], mel_f[pl.ds(9, tiles, stride=2), :]], axis=1
    ).astype(BF16)
    channels = conv_w.shape[1]
    for n in range(0, channels, 256):
        summed = (
            jnp.dot(stacked, conv_w[:, n : n + 256], preferred_element_type=F32)
            + bias[:, n : n + 256]
        )
        feat[:, n : n + 256] = (
            0.5 * summed * (1.0 + lax.erf(summed * (0.5**0.5)))
        ).astype(BF16)

    def enc_copy(b):
        return pltpu.make_async_remote_copy(
            src_ref=sent.at[b],
            dst_ref=wide.at[pl.ds(pl.multiple_of(FRONT + e * tiles, TAIL), tiles)],
            send_sem=enc_send.at[b],
            recv_sem=enc_recv.at[e],
            device_id={"enc": b},
            device_id_type=MESH,
        )

    fronts = {}
    backs = {}
    for t in range(encs):
        low = max(t * tiles, share - FRONT)
        if low < (t + 1) * tiles:
            fronts[t] = (low - t * tiles, (t + 1) * tiles - low, low - (share - FRONT))
        high = min((t + 1) * tiles, DRIFT)
        if high > t * tiles:
            backs[t] = (0, high - t * tiles, FRONT + share + t * tiles)

    def halo_copy(t, b, plan, send_sem, recv_sem, by):
        begin, count, place = plan[t]
        return pltpu.make_async_remote_copy(
            src_ref=sent.at[b, pl.ds(begin, count)],
            dst_ref=wide.at[pl.ds(place, count)],
            send_sem=send_sem.at[b],
            recv_sem=recv_sem.at[t],
            device_id={"seq": s + by, "enc": b},
            device_id_type=MESH,
        )

    def front_copy(t, b):
        return halo_copy(t, b, fronts, front_send, front_recv, 1)

    def back_copy(t, b):
        return halo_copy(t, b, backs, back_send, back_recv, -1)

    def project(j, carry):
        b = lax.rem(e + encs // 2 + j, encs)
        block = jnp.dot(feat[...], proj[b], preferred_element_type=F32).astype(BF16)
        sent[b] = block

        @pl.when(b != e)
        def _():
            enc_copy(b).start()

        @pl.when(b == e)
        def _():
            wide[pl.ds(pl.multiple_of(FRONT + e * tiles, TAIL), tiles), :] = block

        for t in fronts:

            @pl.when((e == t) & (s < owners - 1))
            def _(t=t):
                front_copy(t, b).start()

        for t in backs:

            @pl.when((e == t) & (s > 0))
            def _(t=t):
                back_copy(t, b).start()

        return carry

    lax.fori_loop(0, encs, project, 0)

    low_half = lane_ids < HDIM

    def block_rows(c):
        return pl.ds(pl.multiple_of(c * SPAN, SPAN), SPAN)

    def head_rows(c):
        return pl.ds(pl.multiple_of(c * 8, 8), 8)

    def spread(columns):
        return jnp.concatenate(
            [
                jnp.where(low_half, columns[:, 2 * i : 2 * i + 1], columns[:, 2 * i + 1 : 2 * i + 2])
                for i in range(halves)
            ],
            axis=1,
        )

    def make_weights(c, carry):
        both = lax.dot_general(
            c_map[block_rows(c), :],
            b_map[block_rows(c), :],
            (((1,), (1,)), ((), ())),
            preferred_element_type=F32,
        )
        run = run_s[head_rows(c), :]
        steps = step_s[head_rows(c), :]
        columns = jnp.transpose(run)
        for h in range(heads):
            gap = columns[:, h : h + 1] - run[h : h + 1, :]
            decay = jnp.exp(jnp.where(row_ids >= lane_ids, gap, -1e30))
            weights[c, h * SPAN : (h + 1) * SPAN, :] = (
                decay * both * steps[h : h + 1, :]
            ).astype(BF16)
        return carry

    lax.fori_loop(0, blocks, make_weights, 0)

    def start_of(last):
        return lax.fori_loop(0, last, lambda k, total: total + seg_len[k], jnp.int32(0))

    for j in range(1, encs):
        peer = lax.rem(e + j, encs)
        pltpu.make_async_remote_copy(
            src_ref=sent.at[peer],
            dst_ref=wide.at[pl.ds(pl.multiple_of(FRONT + peer * tiles, TAIL), tiles)],
            send_sem=enc_send.at[peer],
            recv_sem=enc_recv.at[peer],
            device_id={"enc": peer},
            device_id_type=MESH,
        ).wait_recv()

    @pl.when(s > 0)
    def _():
        tail_copy.wait_recv()
        for t in fronts:
            front_copy(t, 0).wait_recv()

    @pl.when(s < owners - 1)
    def _():
        for t in backs:
            back_copy(t, 0).wait_recv()

    @pl.when(s == 0)
    def _():
        wide[0:FRONT, :] = jnp.zeros((FRONT, width), BF16)
        text_tail[...] = jnp.zeros_like(text_tail)

    @pl.when(s == owners - 1)
    def _():
        wide[FRONT + share : FRONT + share + DRIFT, :] = jnp.zeros((DRIFT, width), BF16)

    held = wide.shape[0]
    spare = held - FRONT - share - DRIFT
    if spare:
        wide[held - spare :, :] = jnp.zeros((spare, width), BF16)

    def segment(k):
        return seg_off[k] - s * rows, seg_len[k], start_of(k) - s * share + FRONT

    def placed(first, count, parts, text_rows):
        ids = lax.broadcasted_iota(jnp.int32, (count, SPAN), 0)
        gaps = lax.broadcasted_iota(jnp.int32, (count, SPAN), 1) - ids
        here = first + ids
        shift = jnp.full((count, SPAN), -(1 << 30), jnp.int32)
        for offset, length, start in parts:
            inside = (here >= offset) & (here < offset + length)
            shift = jnp.where(inside, first - offset + start, shift)
        picks = jnp.concatenate(
            [
                jnp.where(gaps == shift - k, 1.0, 0.0).astype(BF16)
                for k in range(0, held, SPAN)
            ],
            axis=1,
        )
        audio = jnp.dot(picks, wide[...], preferred_element_type=F32)
        is_text = jnp.concatenate([shift] * halves, axis=1) < -(1 << 29)
        return jnp.where(is_text, text_rows, audio)

    own = [segment(2 * s), segment(2 * s + 1)]
    prior = 2 * lax.rem(s + owners - 1, owners)
    earlier = [segment(prior), segment(prior + 1)]
    past = placed(-TAIL, TAIL, earlier, text_tail[...].astype(F32))
    x_rows[0:8, :] = jnp.where(s > 0, past[TAIL - 8 :, :], 0.0)
    state[...] = jnp.zeros_like(state)

    def fill(c, carry):
        first = c * PLACED
        x_rows[pl.ds(pl.multiple_of(first + 8, 8), PLACED), :] = placed(
            first,
            PLACED,
            own,
            text[pl.ds(pl.multiple_of(first, PLACED), PLACED), :].astype(F32),
        )
        return carry

    lax.fori_loop(0, rows // PLACED, fill, 0)

    def place(c, before):
        first = c * SPAN
        near = x_rows[pl.ds(pl.multiple_of(first, 8), SPAN + 8), :]
        summed = near[5 : 5 + SPAN] * taps[0:1, :]
        for j in range(1, 4):
            summed = summed + near[5 + j : 5 + j + SPAN] * taps[j : j + 1, :]
        mixed = (summed / (1.0 + jnp.exp(-summed))).astype(BF16)
        xconv[block_rows(c), :] = mixed
        run = spread(jnp.transpose(run_s[head_rows(c), :]))
        steps = spread(jnp.transpose(step_s[head_rows(c), :]))
        last = run[SPAN - 1 : SPAN, :]
        inputs = (mixed.astype(F32) * (steps * jnp.exp(last - run))).astype(BF16)
        added = lax.dot_general(
            b_map[block_rows(c), :], inputs, (((0,), (0,)), ((), ())), preferred_element_type=F32
        )
        now = state[...]
        starts[c] = now.astype(BF16)
        before_s[c] = before
        state[...] = now * jnp.exp(last) + added
        return before + last

    total = lax.fori_loop(0, blocks, place, jnp.zeros((1, width), F32))

    mine[...] = state[...].astype(BF16)
    mine_total[...] = jnp.broadcast_to(total, mine_total.shape)

    def state_copies(to, slot):
        return (
            pltpu.make_async_remote_copy(
                src_ref=mine,
                dst_ref=states.at[slot],
                send_sem=state_send.at[to],
                recv_sem=state_recv.at[slot],
                device_id={"seq": to},
                device_id_type=MESH,
            ),
            pltpu.make_async_remote_copy(
                src_ref=mine_total,
                dst_ref=totals.at[slot],
                send_sem=total_send.at[to],
                recv_sem=total_recv.at[slot],
                device_id={"seq": to},
                device_id_type=MESH,
            ),
        )

    def send_state(to, carry):
        for copy in state_copies(to, s):
            copy.start()
        return carry

    lax.fori_loop(s + 1, owners, send_state, 0)

    skip = params[8:9, :]

    def inner(c, carry):
        mixed = xconv[block_rows(c), :]
        run = spread(jnp.transpose(run_s[head_rows(c), :]))
        wide_y = jnp.dot(weights[c], mixed, preferred_element_type=F32)
        within = jnp.concatenate(
            [
                jnp.where(
                    low_half,
                    wide_y[2 * i * SPAN : (2 * i + 1) * SPAN, i * SPAN : (i + 1) * SPAN],
                    wide_y[(2 * i + 1) * SPAN : (2 * i + 2) * SPAN, i * SPAN : (i + 1) * SPAN],
                )
                for i in range(halves)
            ],
            axis=1,
        )
        carried = jnp.dot(c_map[block_rows(c), :], starts[c], preferred_element_type=F32)
        y_s[block_rows(c), :] = within + carried * jnp.exp(run) + skip * mixed.astype(F32)
        return carry

    lax.fori_loop(0, blocks, inner, 0)

    state[...] = jnp.zeros_like(state)

    def join(r, carry):
        for copy in state_copies(s, r):
            copy.wait_recv()
        state[...] = state[...] * jnp.exp(totals[r][0:1, :]) + states[r].astype(F32)
        return carry

    lax.fori_loop(0, s, join, 0)
    incoming = state[...].astype(BF16)

    def finish(c, carry):
        run = spread(jnp.transpose(run_s[head_rows(c), :]))
        carried = jnp.dot(c_map[block_rows(c), :], incoming, preferred_element_type=F32)
        out[block_rows(c), :] = (
            y_s[block_rows(c), :] + carried * jnp.exp(before_s[c] + run)
        ).astype(BF16)
        return carry

    lax.fori_loop(0, blocks, finish, 0)

    @pl.when(flat < owners * encs - 1)
    def _():
        edge_copy.wait_send()

    @pl.when(s < owners - 1)
    def _():
        tail_copy.wait_send()

    for j in range(1, encs):
        enc_copy(lax.rem(e + j, encs)).wait_send()

    for b in range(encs):
        for t in fronts:

            @pl.when((e == t) & (s < owners - 1))
            def _(t=t, b=b):
                front_copy(t, b).wait_send()

        for t in backs:

            @pl.when((e == t) & (s > 0))
            def _(t=t, b=b):
                back_copy(t, b).wait_send()

    def sent_state(to, carry):
        for copy in state_copies(to, s):
            copy.wait_send()
        return carry

    lax.fori_loop(s + 1, owners, sent_state, 0)


def shards(
    mel_frames,
    conv_weight,
    conv_bias,
    projector,
    seg_offsets,
    seg_lengths,
    text_embed,
    mix_taps,
    input_map,
    output_map,
    step_size,
    decay_log,
    skip_gain,
):
    owners = lax.axis_size("seq")
    encs = lax.axis_size("enc")
    frames, mels = mel_frames.shape
    tiles = frames // 2
    channels = conv_weight.shape[1]
    rows, width = text_embed.shape
    heads = step_size.shape[0]
    blocks = rows // SPAN
    states = input_map.shape[1]
    held = -(-(FRONT + encs * tiles + DRIFT) // SPAN) * SPAN
    rates = jnp.zeros((8, width), F32).at[:heads].set(
        jnp.broadcast_to(jnp.exp(decay_log)[:, None], (heads, width))
    )
    skips = jnp.broadcast_to(
        jnp.broadcast_to(skip_gain[:, None], (heads, HDIM)).reshape(1, width), (8, width)
    )
    params = jnp.concatenate([rates, skips], axis=0)
    vmem = pl.BlockSpec(memory_space=pltpu.VMEM)
    smem = pl.BlockSpec(memory_space=pltpu.SMEM)
    dma = pltpu.SemaphoreType.DMA
    return pl.pallas_call(
        functools.partial(kernel, owners, encs),
        out_shape=jax.ShapeDtypeStruct((rows, width), BF16),
        in_specs=[smem, smem] + [vmem] * 10,
        out_specs=vmem,
        scratch_shapes=[
            pltpu.VMEM((8 + frames, mels), F32),
            pltpu.VMEM((TAIL, mels), BF16),
            pltpu.VMEM((TAIL, width), BF16),
            pltpu.VMEM((tiles, channels), BF16),
            pltpu.VMEM((encs, tiles, width), BF16),
            pltpu.VMEM((held, width), BF16),
            pltpu.VMEM((rows + 8, width), F32),
            pltpu.VMEM((rows, width), BF16),
            pltpu.VMEM((blocks * 8, SPAN), F32),
            pltpu.VMEM((blocks * 8, SPAN), F32),
            pltpu.VMEM((blocks, heads * SPAN, SPAN), BF16),
            pltpu.VMEM((states, width), F32),
            pltpu.VMEM((blocks, states, width), BF16),
            pltpu.VMEM((blocks, 1, width), F32),
            pltpu.VMEM((rows, width), F32),
            pltpu.VMEM((states, width), BF16),
            pltpu.VMEM((8, width), F32),
            pltpu.VMEM((owners, states, width), BF16),
            pltpu.VMEM((owners, 8, width), F32),
            dma((2,)),
            dma((2,)),
            dma((encs,)),
            dma((encs,)),
            dma((encs,)),
            dma((encs,)),
            dma((encs,)),
            dma((encs,)),
            dma((owners,)),
            dma((owners,)),
            dma((owners,)),
            dma((owners,)),
        ],
        compiler_params=pltpu.CompilerParams(
            collective_id=0, has_side_effects=True, vmem_limit_bytes=48 * 1024 * 1024
        ),
    )(
        seg_offsets,
        seg_lengths,
        mel_frames,
        conv_weight,
        conv_bias[None, :],
        jnp.transpose(projector, (1, 0, 2)),
        text_embed,
        mix_taps,
        input_map,
        output_map,
        step_size,
        params,
    )


def solution(mesh):
    return jax.shard_map(
        shards,
        mesh=mesh,
        in_specs=(
            P(("seq", "enc"), None),
            P(),
            P(),
            P(None, None, "head"),
            P(),
            P(),
            P("seq", ("enc", "head")),
            P(None, ("enc", "head")),
            P("seq", "enc"),
            P("seq", "enc"),
            P(("enc", "head"), "seq"),
            P(("enc", "head")),
            P(("enc", "head")),
        ),
        out_specs=P("seq", ("enc", "head")),
        check_vma=False,
    )
```

time: 117 us -> 48.6 us (0.42)
  the two profiles are of different devices: /device:TPU:0 before, /device:TPU:25 now
where the time goes in v1:
time: 48.6 us; the launch traced here: 48.3 us
  Pallas kernels  41.2 us (85%)
  local copies, waits for them, and re-layouts  6.94 us (14%)
    pallas_call x1, Pallas kernels, shards(): pl.pallas_call(functools.partial(kernel, owners, encs), out_shape=jax.Sha...  41.2 us
    unnamed x20, local copies, waits for them, and re-layouts  4.77 us

profile of v1, /device:TPU:25, one launch (start us, length us, event | category | flops | bytes accessed | tf_op | source)
XLA Modules:
  0.0 48.3 jit_solution(9249018532094185225)
XLA Ops:
  0.0 0.7 %exp.3 = f32[4]{0:T(128)S(1)} exponential(f32[4]{0:T(128)} %param.26) | non-fusion elementwise | bytes 32 | tf_op jit(solution)/shard_map/exp | solution.py:520
  0.7 0.7 %broadcast_in_dim.9 = f32[4,64]{1,0:T(4,128)S(1)} broadcast(f32[4]{0:T(128)} %param.27), dimensions={0} | broadcast | bytes 1040 | tf_op jit(solution)/shard_map/broadcast_in_dim | solution.py:523
  1.4 0.1 broadcast_in_dim.10
  1.5 0.7 %broadcast_in_dim.8.bias = f32[1,1280]{1,0:T(1,128)S(1)} reshape(f32[1280]{0:T(1024)} %param.17) | data formatting | bytes 10240 | tf_op jit(solution)/shard_map/broadcast_in_dim | solution.py:575
  2.2 0.1 pad_maximum_fusion.params
  2.3 0.0 copy-start.1
  2.3 0.0 copy-start.2
  2.3 0.0 copy-start.4
  2.3 0.0 copy-start.5
  2.3 0.0 copy-start.6
  2.3 0.0 copy-start.7
  2.3 0.0 copy-start.8
  2.3 3.8 %copy.16 = bf16[1280,4,256]{2,0,1:T(8,128)(2,1)} copy(bf16[1280,4,256]{2,1,0:T(4,128)(2,1)} %param.18) | data formatting | bytes 5242880 | tf_op args[3]
  6.1 0.0 copy-done
  6.1 0.0 copy-done.1
  6.1 0.0 copy-done.2
  6.1 0.0 copy-done.3
  6.1 0.0 copy-done.4
  6.1 0.0 copy-done.5
  6.1 0.0 copy-done.6
  6.1 0.0 copy-done.7
  6.1 0.0 copy-done.8
  6.2 41.2 %shard_map.127 = bf16[2048,256]{1,0:T(8,128)(2,1)S(1)} custom-call(s32[8]{0:T(128)S(1)} %copy-done.7, s32[8]{0:T(128)S(1)} %copy-done.8, bf16[512,128]{1,0:T(8,128)(2,1)S(1)} %copy-done.4, bf16[384,1280]{1,0:T(8,128)(2,1)S(1)} %copy-done.1, f32[1,1280]{1,0:T(1,128)S(1)} %broadcast_in_dim.8.bias, bf16[4,1280,256]{2,1,0:T(8,128)(2,1)} %bitcast.3, ...), custom_call_target="tpu_custom_call" | custom-call | tf_op jit(solution)/shard_map/pallas_call | solution.py:529
  47.4 1.0 %copy.18 = bf16[2048,256]{1,0:T(8,128)(2,1)} copy(bf16[2048,256]{1,0:T(8,128)(2,1)S(1)} %shard_map.127) | data formatting | bytes 2097152
  (4 shorter events, 0.0 us)
Async XLA Ops:
  2.3 3.8 %copy-start = (bf16[2048,256]{1,0:T(8,128)(2,1)S(1)}, bf16[2048,256]{1,0:T(8,128)(2,1)}, u32[]{:S(2)}) copy-start(bf16[2048,256]{1,0:T(8,128)(2,1)} %text.1) | copy-start | bytes 3145732
  2.3 3.8 %copy-start.1 = (bf16[384,1280]{1,0:T(8,128)(2,1)S(1)}, bf16[384,1280]{1,0:T(8,128)(2,1)}, u32[]{:S(2)}) copy-start(bf16[384,1280]{1,0:T(8,128)(2,1)} %conv_w.1) | copy-start | bytes 2949124
  2.3 3.8 %copy-start.2 = (bf16[2048,128]{1,0:T(8,128)(2,1)S(1)}, bf16[2048,128]{1,0:T(8,128)(2,1)}, u32[]{:S(2)}) copy-start(bf16[2048,128]{1,0:T(8,128)(2,1)} %b_map.1) | copy-start | bytes 1572868
  2.3 3.8 %copy-start.3 = (bf16[2048,128]{1,0:T(8,128)(2,1)S(1)}, bf16[2048,128]{1,0:T(8,128)(2,1)}, u32[]{:S(2)}) copy-start(bf16[2048,128]{1,0:T(8,128)(2,1)} %c_map.1) | copy-start | bytes 1572868
  2.3 3.8 %copy-start.4 = (bf16[512,128]{1,0:T(8,128)(2,1)S(1)}, bf16[512,128]{1,0:T(8,128)(2,1)}, u32[]{:S(2)}) copy-start(bf16[512,128]{1,0:T(8,128)(2,1)} %mel.1) | copy-start | bytes 393220
  2.3 3.8 %copy-start.5 = (f32[4,2048]{1,0:T(4,128)S(1)}, f32[4,2048]{1,0:T(4,128)}, u32[]{:S(2)}) copy-start(f32[4,2048]{1,0:T(4,128)} %step.1) | copy-start | bytes 98308
  2.3 3.8 %copy-start.6 = (f32[4,256]{1,0:T(4,128)S(1)}, f32[4,256]{1,0:T(4,128)}, u32[]{:S(2)}) copy-start(f32[4,256]{1,0:T(4,128)} %taps.1) | copy-start | bytes 12292
  2.3 3.8 %copy-start.7 = (s32[8]{0:T(128)S(1)}, s32[8]{0:T(128)}, u32[]{:S(2)}) copy-start(s32[8]{0:T(128)} %seg_off.1) | copy-start | bytes 100
  2.3 3.8 %copy-start.8 = (s32[8]{0:T(128)S(1)}, s32[8]{0:T(128)}, u32[]{:S(2)}) copy-start(s32[8]{0:T(128)} %seg_len.1) | copy-start | bytes 100

commit v2 on v1

--- a/solution.py
+++ b/solution.py
@@ -32,7 +32,8 @@
     b_map,
     c_map,
     step,
-    params,
+    decay_log,
+    skip_gain,
     out,
     mel_f,
     edge,
@@ -45,9 +46,12 @@
     step_s,
     run_s,
     weights,
+    grown,
+    tails,
     state,
     starts,
     before_s,
+    lasts,
     y_s,
     mine,
     mine_total,
@@ -135,7 +139,10 @@
     step_s[...] = jnp.zeros_like(step_s)
     for c in range(blocks):
         step_s[c * 8 : c * 8 + heads, :] = step[:, c * SPAN : (c + 1) * SPAN]
-    rate = params[0:8, 0:SPAN]
+    head_ids = lax.broadcasted_iota(jnp.int32, (8, SPAN), 0)
+    rate = jnp.zeros((8, SPAN), F32)
+    for h in range(heads):
+        rate = jnp.where(head_ids == h, jnp.exp(jnp.full((8, SPAN), decay_log[h], F32)), rate)
     logs = -(step_s[...].reshape(blocks, 8, SPAN) * rate[None]).reshape(blocks * 8, SPAN)
     row_ids = lax.broadcasted_iota(jnp.int32, (SPAN, SPAN), 0)
     lane_ids = lax.broadcasted_iota(jnp.int32, (SPAN, SPAN), 1)
@@ -173,7 +180,9 @@
     for n in range(0, channels, 256):
         summed = (
             jnp.dot(stacked, conv_w[:, n : n + 256], preferred_element_type=F32)
-            + bias[:, n : n + 256]
+            + jnp.concatenate(
+                [bias[k : k + 1, :] for k in range(n // SPAN, (n + 256) // SPAN)], axis=1
+            )
         )
         feat[:, n : n + 256] = (
             0.5 * summed * (1.0 + lax.erf(summed * (0.5**0.5)))
@@ -278,9 +287,14 @@
             weights[c, h * SPAN : (h + 1) * SPAN, :] = (
                 decay * both * steps[h : h + 1, :]
             ).astype(BF16)
-        return carry
-
-    lax.fori_loop(0, blocks, make_weights, 0)
+        run_wide = spread(columns)
+        last = run_wide[SPAN - 1 : SPAN, :]
+        grown[block_rows(c), :] = jnp.exp(run_wide)
+        tails[block_rows(c), :] = spread(jnp.transpose(steps)) * jnp.exp(last - run_wide)
+        lasts[c] = last
+        return carry
+
+    lax.fori_loop(0, blocks, make_weights, 0, unroll=2)
 
     def start_of(last):
         return lax.fori_loop(0, last, lambda k, total: total + seg_len[k], jnp.int32(0))
@@ -370,20 +384,18 @@
             summed = summed + near[5 + j : 5 + j + SPAN] * taps[j : j + 1, :]
         mixed = (summed / (1.0 + jnp.exp(-summed))).astype(BF16)
         xconv[block_rows(c), :] = mixed
-        run = spread(jnp.transpose(run_s[head_rows(c), :]))
-        steps = spread(jnp.transpose(step_s[head_rows(c), :]))
-        last = run[SPAN - 1 : SPAN, :]
-        inputs = (mixed.astype(F32) * (steps * jnp.exp(last - run))).astype(BF16)
+        last = lasts[c]
+        inputs = (mixed.astype(F32) * tails[block_rows(c), :]).astype(BF16)
         added = lax.dot_general(
             b_map[block_rows(c), :], inputs, (((0,), (0,)), ((), ())), preferred_element_type=F32
         )
         now = state[...]
         starts[c] = now.astype(BF16)
-        before_s[c] = before
+        before_s[c] = jnp.exp(before)
         state[...] = now * jnp.exp(last) + added
         return before + last
 
-    total = lax.fori_loop(0, blocks, place, jnp.zeros((1, width), F32))
+    total = lax.fori_loop(0, blocks, place, jnp.zeros((1, width), F32), unroll=2)
 
     mine[...] = state[...].astype(BF16)
     mine_total[...] = jnp.broadcast_to(total, mine_total.shape)
@@ -415,11 +427,16 @@
 
     lax.fori_loop(s + 1, owners, send_state, 0)
 
-    skip = params[8:9, :]
+    skip = jnp.concatenate(
+        [
+            jnp.where(low_half[0:1, :], skip_gain[2 * i], skip_gain[2 * i + 1])
+            for i in range(halves)
+        ],
+        axis=1,
+    )
 
     def inner(c, carry):
         mixed = xconv[block_rows(c), :]
-        run = spread(jnp.transpose(run_s[head_rows(c), :]))
         wide_y = jnp.dot(weights[c], mixed, preferred_element_type=F32)
         within = jnp.concatenate(
             [
@@ -433,10 +450,12 @@
             axis=1,
         )
         carried = jnp.dot(c_map[block_rows(c), :], starts[c], preferred_element_type=F32)
-        y_s[block_rows(c), :] = within + carried * jnp.exp(run) + skip * mixed.astype(F32)
-        return carry
-
-    lax.fori_loop(0, blocks, inner, 0)
+        y_s[block_rows(c), :] = (
+            within + carried * grown[block_rows(c), :] + skip * mixed.astype(F32)
+        )
+        return carry
+
+    lax.fori_loop(0, blocks, inner, 0, unroll=2)
 
     state[...] = jnp.zeros_like(state)
 
@@ -450,14 +469,13 @@
     incoming = state[...].astype(BF16)
 
     def finish(c, carry):
-        run = spread(jnp.transpose(run_s[head_rows(c), :]))
         carried = jnp.dot(c_map[block_rows(c), :], incoming, preferred_element_type=F32)
         out[block_rows(c), :] = (
-            y_s[block_rows(c), :] + carried * jnp.exp(before_s[c] + run)
+            y_s[block_rows(c), :] + carried * before_s[c] * grown[block_rows(c), :]
         ).astype(BF16)
         return carry
 
-    lax.fori_loop(0, blocks, finish, 0)
+    lax.fori_loop(0, blocks, finish, 0, unroll=4)
 
     @pl.when(flat < owners * encs - 1)
     def _():
@@ -516,20 +534,13 @@
     blocks = rows // SPAN
     states = input_map.shape[1]
     held = -(-(FRONT + encs * tiles + DRIFT) // SPAN) * SPAN
-    rates = jnp.zeros((8, width), F32).at[:heads].set(
-        jnp.broadcast_to(jnp.exp(decay_log)[:, None], (heads, width))
-    )
-    skips = jnp.broadcast_to(
-        jnp.broadcast_to(skip_gain[:, None], (heads, HDIM)).reshape(1, width), (8, width)
-    )
-    params = jnp.concatenate([rates, skips], axis=0)
     vmem = pl.BlockSpec(memory_space=pltpu.VMEM)
     smem = pl.BlockSpec(memory_space=pltpu.SMEM)
     dma = pltpu.SemaphoreType.DMA
     return pl.pallas_call(
         functools.partial(kernel, owners, encs),
         out_shape=jax.ShapeDtypeStruct((rows, width), BF16),
-        in_specs=[smem, smem] + [vmem] * 10,
+        in_specs=[smem, smem] + [vmem] * 9 + [smem, smem],
         out_specs=vmem,
         scratch_shapes=[
             pltpu.VMEM((8 + frames, mels), F32),
@@ -543,8 +554,11 @@
             pltpu.VMEM((blocks * 8, SPAN), F32),
             pltpu.VMEM((blocks * 8, SPAN), F32),
             pltpu.VMEM((blocks, heads * SPAN, SPAN), BF16),
+            pltpu.VMEM((rows, width), F32),
+            pltpu.VMEM((rows, width), F32),
             pltpu.VMEM((states, width), F32),
             pltpu.VMEM((blocks, states, width), BF16),
+            pltpu.VMEM((blocks, 1, width), F32),
             pltpu.VMEM((blocks, 1, width), F32),
             pltpu.VMEM((rows, width), F32),
             pltpu.VMEM((states, width), BF16),
@@ -572,14 +586,15 @@
         seg_lengths,
         mel_frames,
         conv_weight,
-        conv_bias[None, :],
+        conv_bias.reshape(channels // SPAN, SPAN),
         jnp.transpose(projector, (1, 0, 2)),
         text_embed,
         mix_taps,
         input_map,
         output_map,
         step_size,
-        params,
+        decay_log,
+        skip_gain,
     )
 
 

time: 48.6 us -> 38.6 us (0.79)
  Pallas kernels: 41.2 us -> 33.6 us
  local copies, waits for them, and re-layouts: 6.94 us -> 4.77 us
    pallas_call x1, Pallas kernels: 41.2 us -> 33.6 us  [shards(): pl.pallas_call(functools.partial(kernel, owners, encs), out_shape=jax.Sha...]
    broadcast_in_dim x4 -> x0, local copies, waits for them, and re-layouts: 1.51 us -> none  [the longest x1 0.73 us: shards(): jnp.broadcast_to(skip_gain[:, None], (heads, HDIM)).reshape(1, width)]
    exp x1 -> x0, local copies, waits for them, and re-layouts: 0.66 us -> none  [shards(): jnp.exp(decay_log)[:, None]]
    unnamed x20 -> x26, local copies, waits for them, and re-layouts: 4.77 us -> 4.77 us
where the time goes in v2:
time: 38.6 us; the launch traced here: 38.5 us
  Pallas kernels  33.6 us (87%)
  local copies, waits for them, and re-layouts  4.77 us (12%)
    pallas_call x1, Pallas kernels, shards(): pl.pallas_call(functools.partial(kernel, owners, encs), out_shape=jax.Sha...  33.6 us
    unnamed x26, local copies, waits for them, and re-layouts  4.77 us

profile of v2, /device:TPU:25, one launch (start us, length us, event | category | flops | bytes accessed | tf_op | source)
XLA Modules:
  0.0 38.5 jit_solution(3879788843343831809)
XLA Ops:
  0.0 0.0 copy-start.3
  0.0 0.0 copy-start.4
  0.0 0.0 copy-start.5
  0.0 0.0 copy-start.6
  0.0 0.0 copy-start.7
  0.1 0.0 copy-start.8
  0.1 0.0 copy-start.9
  0.1 0.0 copy-start.10
  0.1 0.0 copy-start.11
  0.1 3.8 %copy.16 = bf16[1280,4,256]{2,0,1:T(8,128)(2,1)} copy(bf16[1280,4,256]{2,1,0:T(4,128)(2,1)} %param.16) | data formatting | bytes 5242880 | tf_op args[3]
  3.9 0.0 copy-done
  3.9 0.0 copy-done.1
  3.9 0.0 copy-done.2
  3.9 0.0 copy-done.3
  3.9 0.0 copy-done.4
  3.9 0.0 copy-done.5
  3.9 0.0 copy-done.6
  3.9 0.0 copy-done.7
  3.9 0.0 copy-done.8
  3.9 0.0 copy-done.9
  3.9 0.0 copy-done.10
  3.9 0.0 copy-done.11
  4.0 33.6 %shard_map.127 = bf16[2048,256]{1,0:T(8,128)(2,1)S(1)} custom-call(s32[8]{0:T(128)S(1)} %copy-done.8, s32[8]{0:T(128)S(1)} %copy-done.9, bf16[512,128]{1,0:T(8,128)(2,1)S(1)} %copy-done.4, bf16[384,1280]{1,0:T(8,128)(2,1)S(1)} %copy-done.1, f32[10,128]{1,0:T(8,128)S(1)} %bitcast.4, bf16[4,1280,256]{2,1,0:T(8,128)(2,1)} %bitcast.5, ...), custom_call_target="tpu_custom_call" | custom-call | tf_op jit(solution)/shard_map/pallas_call | solution.py:540
  37.5 1.0 %copy.18 = bf16[2048,256]{1,0:T(8,128)(2,1)} copy(bf16[2048,256]{1,0:T(8,128)(2,1)S(1)} %shard_map.127) | data formatting | bytes 2097152
  (3 shorter events, 0.0 us)
Async XLA Ops:
  0.0 3.9 %copy-start = (bf16[2048,256]{1,0:T(8,128)(2,1)S(1)}, bf16[2048,256]{1,0:T(8,128)(2,1)}, u32[]{:S(2)}) copy-start(bf16[2048,256]{1,0:T(8,128)(2,1)} %text.1) | copy-start | bytes 3145732
  0.0 3.9 %copy-start.1 = (bf16[384,1280]{1,0:T(8,128)(2,1)S(1)}, bf16[384,1280]{1,0:T(8,128)(2,1)}, u32[]{:S(2)}) copy-start(bf16[384,1280]{1,0:T(8,128)(2,1)} %conv_w.1) | copy-start | bytes 2949124
  0.0 3.9 %copy-start.2 = (bf16[2048,128]{1,0:T(8,128)(2,1)S(1)}, bf16[2048,128]{1,0:T(8,128)(2,1)}, u32[]{:S(2)}) copy-start(bf16[2048,128]{1,0:T(8,128)(2,1)} %b_map.1) | copy-start | bytes 1572868
  0.0 3.9 %copy-start.3 = (bf16[2048,128]{1,0:T(8,128)(2,1)S(1)}, bf16[2048,128]{1,0:T(8,128)(2,1)}, u32[]{:S(2)}) copy-start(bf16[2048,128]{1,0:T(8,128)(2,1)} %c_map.1) | copy-start | bytes 1572868
  0.0 3.9 %copy-start.4 = (bf16[512,128]{1,0:T(8,128)(2,1)S(1)}, bf16[512,128]{1,0:T(8,128)(2,1)}, u32[]{:S(2)}) copy-start(bf16[512,128]{1,0:T(8,128)(2,1)} %mel.1) | copy-start | bytes 393220
  0.0 3.9 %copy-start.5 = (f32[4,2048]{1,0:T(4,128)S(1)}, f32[4,2048]{1,0:T(4,128)}, u32[]{:S(2)}) copy-start(f32[4,2048]{1,0:T(4,128)} %step.1) | copy-start | bytes 98308
  0.0 3.9 %copy-start.6 = (f32[1280]{0:T(1024)S(1)}, f32[1280]{0:T(1024)}, u32[]{:S(2)}) copy-start(f32[1280]{0:T(1024)} %param.15) | copy-start | bytes 15364
  0.0 3.9 %copy-start.7 = (f32[4,256]{1,0:T(4,128)S(1)}, f32[4,256]{1,0:T(4,128)}, u32[]{:S(2)}) copy-start(f32[4,256]{1,0:T(4,128)} %taps.1) | copy-start | bytes 12292
  0.1 3.9 %copy-start.8 = (s32[8]{0:T(128)S(1)}, s32[8]{0:T(128)}, u32[]{:S(2)}) copy-start(s32[8]{0:T(128)} %seg_off.1) | copy-start | bytes 100
  0.1 3.9 %copy-start.9 = (s32[8]{0:T(128)S(1)}, s32[8]{0:T(128)}, u32[]{:S(2)}) copy-start(s32[8]{0:T(128)} %seg_len.1) | copy-start | bytes 100
  0.1 3.9 %copy-start.10 = (f32[4]{0:T(128)S(1)}, f32[4]{0:T(128)}, u32[]{:S(2)}) copy-start(f32[4]{0:T(128)} %decay_log.1) | copy-start | bytes 52
  0.1 3.9 %copy-start.11 = (f32[4]{0:T(128)S(1)}, f32[4]{0:T(128)}, u32[]{:S(2)}) copy-start(f32[4]{0:T(128)} %skip_gain.1) | copy-start | bytes 52

commit v3 on v2

--- a/solution.py
+++ b/solution.py
@@ -294,7 +294,7 @@
         lasts[c] = last
         return carry
 
-    lax.fori_loop(0, blocks, make_weights, 0, unroll=2)
+    lax.fori_loop(0, blocks, make_weights, 0, unroll=4)
 
     def start_of(last):
         return lax.fori_loop(0, last, lambda k, total: total + seg_len[k], jnp.int32(0))
@@ -374,7 +374,7 @@
         )
         return carry
 
-    lax.fori_loop(0, rows // PLACED, fill, 0)
+    lax.fori_loop(0, rows // PLACED, fill, 0, unroll=2)
 
     def place(c, before):
         first = c * SPAN
@@ -395,7 +395,7 @@
         state[...] = now * jnp.exp(last) + added
         return before + last
 
-    total = lax.fori_loop(0, blocks, place, jnp.zeros((1, width), F32), unroll=2)
+    total = lax.fori_loop(0, blocks, place, jnp.zeros((1, width), F32), unroll=4)
 
     mine[...] = state[...].astype(BF16)
     mine_total[...] = jnp.broadcast_to(total, mine_total.shape)
@@ -455,7 +455,7 @@
         )
         return carry
 
-    lax.fori_loop(0, blocks, inner, 0, unroll=2)
+    lax.fori_loop(0, blocks, inner, 0, unroll=4)
 
     state[...] = jnp.zeros_like(state)
 
@@ -475,7 +475,7 @@
         ).astype(BF16)
         return carry
 
-    lax.fori_loop(0, blocks, finish, 0, unroll=4)
+    lax.fori_loop(0, blocks, finish, 0, unroll=8)
 
     @pl.when(flat < owners * encs - 1)
     def _():

time: 38.6 us -> 37.2 us (0.964)
  Pallas kernels: 33.6 us -> 32.2 us
    pallas_call x1, Pallas kernels: 33.6 us -> 32.2 us  [shards(): pl.pallas_call(functools.partial(kernel, owners, encs), out_shape=jax.Sha...]
where the time goes in v3:
time: 37.2 us; the launch traced here: 37.1 us
  Pallas kernels  32.2 us (87%)
  local copies, waits for them, and re-layouts  4.77 us (13%)
    pallas_call x1, Pallas kernels, shards(): pl.pallas_call(functools.partial(kernel, owners, encs), out_shape=jax.Sha...  32.2 us
    unnamed x26, local copies, waits for them, and re-layouts  4.77 us

profile of v3, /device:TPU:25, one launch (start us, length us, event | category | flops | bytes accessed | tf_op | source)
XLA Modules:
  0.0 37.1 jit_solution(5390561320972436049)
XLA Ops:
  0.0 0.0 copy-start.3
  0.0 0.0 copy-start.4
  0.0 0.0 copy-start.5
  0.0 0.0 copy-start.6
  0.0 0.0 copy-start.7
  0.1 0.0 copy-start.8
  0.1 0.0 copy-start.9
  0.1 0.0 copy-start.10
  0.1 0.0 copy-start.11
  0.1 3.8 %copy.16 = bf16[1280,4,256]{2,0,1:T(8,128)(2,1)} copy(bf16[1280,4,256]{2,1,0:T(4,128)(2,1)} %param.16) | data formatting | bytes 5242880 | tf_op args[3]
  3.9 0.0 copy-done
  3.9 0.0 copy-done.1
  3.9 0.0 copy-done.2
  3.9 0.0 copy-done.3
  3.9 0.0 copy-done.4
  3.9 0.0 copy-done.5
  3.9 0.0 copy-done.6
  3.9 0.0 copy-done.7
  3.9 0.0 copy-done.8
  3.9 0.0 copy-done.9
  3.9 0.0 copy-done.10
  3.9 0.0 copy-done.11
  4.0 32.2 %shard_map.127 = bf16[2048,256]{1,0:T(8,128)(2,1)S(1)} custom-call(s32[8]{0:T(128)S(1)} %copy-done.8, s32[8]{0:T(128)S(1)} %copy-done.9, bf16[512,128]{1,0:T(8,128)(2,1)S(1)} %copy-done.4, bf16[384,1280]{1,0:T(8,128)(2,1)S(1)} %copy-done.1, f32[10,128]{1,0:T(8,128)S(1)} %bitcast.4, bf16[4,1280,256]{2,1,0:T(8,128)(2,1)} %bitcast.5, ...), custom_call_target="tpu_custom_call" | custom-call | tf_op jit(solution)/shard_map/pallas_call | solution.py:540
  36.1 1.0 %copy.18 = bf16[2048,256]{1,0:T(8,128)(2,1)} copy(bf16[2048,256]{1,0:T(8,128)(2,1)S(1)} %shard_map.127) | data formatting | bytes 2097152
  (3 shorter events, 0.0 us)
Async XLA Ops:
  0.0 3.9 %copy-start = (bf16[2048,256]{1,0:T(8,128)(2,1)S(1)}, bf16[2048,256]{1,0:T(8,128)(2,1)}, u32[]{:S(2)}) copy-start(bf16[2048,256]{1,0:T(8,128)(2,1)} %text.1) | copy-start | bytes 3145732
  0.0 3.9 %copy-start.1 = (bf16[384,1280]{1,0:T(8,128)(2,1)S(1)}, bf16[384,1280]{1,0:T(8,128)(2,1)}, u32[]{:S(2)}) copy-start(bf16[384,1280]{1,0:T(8,128)(2,1)} %conv_w.1) | copy-start | bytes 2949124
  0.0 3.9 %copy-start.2 = (bf16[2048,128]{1,0:T(8,128)(2,1)S(1)}, bf16[2048,128]{1,0:T(8,128)(2,1)}, u32[]{:S(2)}) copy-start(bf16[2048,128]{1,0:T(8,128)(2,1)} %b_map.1) | copy-start | bytes 1572868
  0.0 3.9 %copy-start.3 = (bf16[2048,128]{1,0:T(8,128)(2,1)S(1)}, bf16[2048,128]{1,0:T(8,128)(2,1)}, u32[]{:S(2)}) copy-start(bf16[2048,128]{1,0:T(8,128)(2,1)} %c_map.1) | copy-start | bytes 1572868
  0.0 3.9 %copy-start.4 = (bf16[512,128]{1,0:T(8,128)(2,1)S(1)}, bf16[512,128]{1,0:T(8,128)(2,1)}, u32[]{:S(2)}) copy-start(bf16[512,128]{1,0:T(8,128)(2,1)} %mel.1) | copy-start | bytes 393220
  0.0 3.9 %copy-start.5 = (f32[4,2048]{1,0:T(4,128)S(1)}, f32[4,2048]{1,0:T(4,128)}, u32[]{:S(2)}) copy-start(f32[4,2048]{1,0:T(4,128)} %step.1) | copy-start | bytes 98308
  0.0 3.9 %copy-start.6 = (f32[1280]{0:T(1024)S(1)}, f32[1280]{0:T(1024)}, u32[]{:S(2)}) copy-start(f32[1280]{0:T(1024)} %param.15) | copy-start | bytes 15364
  0.0 3.9 %copy-start.7 = (f32[4,256]{1,0:T(4,128)S(1)}, f32[4,256]{1,0:T(4,128)}, u32[]{:S(2)}) copy-start(f32[4,256]{1,0:T(4,128)} %taps.1) | copy-start | bytes 12292
  0.1 3.9 %copy-start.8 = (s32[8]{0:T(128)S(1)}, s32[8]{0:T(128)}, u32[]{:S(2)}) copy-start(s32[8]{0:T(128)} %seg_off.1) | copy-start | bytes 100
  0.1 3.9 %copy-start.9 = (s32[8]{0:T(128)S(1)}, s32[8]{0:T(128)}, u32[]{:S(2)}) copy-start(s32[8]{0:T(128)} %seg_len.1) | copy-start | bytes 100
  0.1 3.9 %copy-start.10 = (f32[4]{0:T(128)S(1)}, f32[4]{0:T(128)}, u32[]{:S(2)}) copy-start(f32[4]{0:T(128)} %decay_log.1) | copy-start | bytes 52
  0.1 3.9 %copy-start.11 = (f32[4]{0:T(128)S(1)}, f32[4]{0:T(128)}, u32[]{:S(2)}) copy-start(f32[4]{0:T(128)} %skip_gain.1) | copy-start | bytes 52

commit v4 on v3

--- a/solution.py
+++ b/solution.py
@@ -226,7 +226,7 @@
         return halo_copy(t, b, backs, back_send, back_recv, -1)
 
     def project(j, carry):
-        b = lax.rem(e + encs // 2 + j, encs)
+        b = lax.rem(e + j, encs)
         block = jnp.dot(feat[...], proj[b], preferred_element_type=F32).astype(BF16)
         sent[b] = block
 
@@ -252,7 +252,9 @@
 
         return carry
 
-    lax.fori_loop(0, encs, project, 0)
+    order = sorted(range(1, encs), key=lambda j: (j < encs // 2, j)) + [0]
+    for j in order:
+        project(j, 0)
 
     low_half = lane_ids < HDIM
 
@@ -294,7 +296,7 @@
         lasts[c] = last
         return carry
 
-    lax.fori_loop(0, blocks, make_weights, 0, unroll=4)
+    lax.fori_loop(0, blocks, make_weights, 0, unroll=8)
 
     def start_of(last):
         return lax.fori_loop(0, last, lambda k, total: total + seg_len[k], jnp.int32(0))
@@ -374,7 +376,7 @@
         )
         return carry
 
-    lax.fori_loop(0, rows // PLACED, fill, 0, unroll=2)
+    lax.fori_loop(0, rows // PLACED, fill, 0, unroll=4)
 
     def place(c, before):
         first = c * SPAN

time: 37.2 us -> 35.9 us (0.965)
  Pallas kernels: 32.2 us -> 30.8 us
    pallas_call x1, Pallas kernels: 32.2 us -> 30.8 us  [shards(): pl.pallas_call(functools.partial(kernel, owners, encs), out_shape=jax.Sha...]
where the time goes in v4:
time: 35.9 us; the launch traced here: 35.7 us
  Pallas kernels  30.8 us (86%)
  local copies, waits for them, and re-layouts  4.77 us (13%)
    pallas_call x1, Pallas kernels, shards(): pl.pallas_call(functools.partial(kernel, owners, encs), out_shape=jax.Sha...  30.8 us
    unnamed x26, local copies, waits for them, and re-layouts  4.77 us

profile of v4, /device:TPU:25, one launch (start us, length us, event | category | flops | bytes accessed | tf_op | source)
XLA Modules:
  0.0 35.7 jit_solution(5812771544015770789)
XLA Ops:
  0.0 0.0 copy-start.3
  0.0 0.0 copy-start.4
  0.0 0.0 copy-start.5
  0.0 0.0 copy-start.6
  0.0 0.0 copy-start.7
  0.1 0.0 copy-start.8
  0.1 0.0 copy-start.9
  0.1 0.0 copy-start.10
  0.1 0.0 copy-start.11
  0.1 3.8 %copy.16 = bf16[1280,4,256]{2,0,1:T(8,128)(2,1)} copy(bf16[1280,4,256]{2,1,0:T(4,128)(2,1)} %param.16) | data formatting | bytes 5242880 | tf_op args[3]
  3.9 0.0 copy-done
  3.9 0.0 copy-done.1
  3.9 0.0 copy-done.2
  3.9 0.0 copy-done.3
  3.9 0.0 copy-done.4
  3.9 0.0 copy-done.5
  3.9 0.0 copy-done.6
  3.9 0.0 copy-done.7
  3.9 0.0 copy-done.8
  3.9 0.0 copy-done.9
  3.9 0.0 copy-done.10
  3.9 0.0 copy-done.11
  4.0 30.8 %shard_map.127 = bf16[2048,256]{1,0:T(8,128)(2,1)S(1)} custom-call(s32[8]{0:T(128)S(1)} %copy-done.8, s32[8]{0:T(128)S(1)} %copy-done.9, bf16[512,128]{1,0:T(8,128)(2,1)S(1)} %copy-done.4, bf16[384,1280]{1,0:T(8,128)(2,1)S(1)} %copy-done.1, f32[10,128]{1,0:T(8,128)S(1)} %bitcast.4, bf16[4,1280,256]{2,1,0:T(8,128)(2,1)} %bitcast.5, ...), custom_call_target="tpu_custom_call" | custom-call | tf_op jit(solution)/shard_map/pallas_call | solution.py:542
  34.8 1.0 %copy.18 = bf16[2048,256]{1,0:T(8,128)(2,1)} copy(bf16[2048,256]{1,0:T(8,128)(2,1)S(1)} %shard_map.127) | data formatting | bytes 2097152
  (3 shorter events, 0.0 us)
Async XLA Ops:
  0.0 3.9 %copy-start = (bf16[2048,256]{1,0:T(8,128)(2,1)S(1)}, bf16[2048,256]{1,0:T(8,128)(2,1)}, u32[]{:S(2)}) copy-start(bf16[2048,256]{1,0:T(8,128)(2,1)} %text.1) | copy-start | bytes 3145732
  0.0 3.9 %copy-start.1 = (bf16[384,1280]{1,0:T(8,128)(2,1)S(1)}, bf16[384,1280]{1,0:T(8,128)(2,1)}, u32[]{:S(2)}) copy-start(bf16[384,1280]{1,0:T(8,128)(2,1)} %conv_w.1) | copy-start | bytes 2949124
  0.0 3.9 %copy-start.2 = (bf16[2048,128]{1,0:T(8,128)(2,1)S(1)}, bf16[2048,128]{1,0:T(8,128)(2,1)}, u32[]{:S(2)}) copy-start(bf16[2048,128]{1,0:T(8,128)(2,1)} %b_map.1) | copy-start | bytes 1572868
  0.0 3.9 %copy-start.3 = (bf16[2048,128]{1,0:T(8,128)(2,1)S(1)}, bf16[2048,128]{1,0:T(8,128)(2,1)}, u32[]{:S(2)}) copy-start(bf16[2048,128]{1,0:T(8,128)(2,1)} %c_map.1) | copy-start | bytes 1572868
  0.0 3.9 %copy-start.4 = (bf16[512,128]{1,0:T(8,128)(2,1)S(1)}, bf16[512,128]{1,0:T(8,128)(2,1)}, u32[]{:S(2)}) copy-start(bf16[512,128]{1,0:T(8,128)(2,1)} %mel.1) | copy-start | bytes 393220
  0.0 3.9 %copy-start.5 = (f32[4,2048]{1,0:T(4,128)S(1)}, f32[4,2048]{1,0:T(4,128)}, u32[]{:S(2)}) copy-start(f32[4,2048]{1,0:T(4,128)} %step.1) | copy-start | bytes 98308
  0.0 3.9 %copy-start.6 = (f32[1280]{0:T(1024)S(1)}, f32[1280]{0:T(1024)}, u32[]{:S(2)}) copy-start(f32[1280]{0:T(1024)} %param.15) | copy-start | bytes 15364
  0.0 3.9 %copy-start.7 = (f32[4,256]{1,0:T(4,128)S(1)}, f32[4,256]{1,0:T(4,128)}, u32[]{:S(2)}) copy-start(f32[4,256]{1,0:T(4,128)} %taps.1) | copy-start | bytes 12292
  0.1 3.9 %copy-start.8 = (s32[8]{0:T(128)S(1)}, s32[8]{0:T(128)}, u32[]{:S(2)}) copy-start(s32[8]{0:T(128)} %seg_off.1) | copy-start | bytes 100
  0.1 3.9 %copy-start.9 = (s32[8]{0:T(128)S(1)}, s32[8]{0:T(128)}, u32[]{:S(2)}) copy-start(s32[8]{0:T(128)} %seg_len.1) | copy-start | bytes 100
  0.1 3.9 %copy-start.10 = (f32[4]{0:T(128)S(1)}, f32[4]{0:T(128)}, u32[]{:S(2)}) copy-start(f32[4]{0:T(128)} %decay_log.1) | copy-start | bytes 52
  0.1 3.9 %copy-start.11 = (f32[4]{0:T(128)S(1)}, f32[4]{0:T(128)}, u32[]{:S(2)}) copy-start(f32[4]{0:T(128)} %skip_gain.1) | copy-start | bytes 52
